TPU v7x, 512 devices: a whole 4x4x16 slice. The times are simulated.
512 devices in a mesh: date: 128 (over z, y, x_lo), az: 4 (over x_hi, core).
Axes of the slice: x: 4 (x_hi: 2, x_lo: 2; x = x_hi * 2 + x_lo), y: 4, z: 16, core: 2. Of those that a mesh axis runs over, the one named last changes fastest.
Arguments:
- slabs: float32 [128, 2, 128, 2048], P('date', None, 'az'), may hold values from -6 to 6
Outputs:
- interferos: float32 [5, 2, 128, 32, 128], P(None, None, 'date', 'az')
- coherence: float32 [5, 128, 32, 128], P(None, 'date', 'az')
All inputs are finite; a program needn't handle non-finite values.
Results may differ from a plain program's by a relative error of at most 0.0003.
Values sent between devices are 32-bit elements; how exact they have to be, the bound alone decides.
No kernel may reach another device: no remote copies, remote signals or barrier semaphores. Data moves between devices by JAX's collectives and lax.ppermute only.
A program may use at most 64 MiB of HBM per device.

v0:
```python
import jax
import jax.numpy as jnp
from jax import lax
from jax.experimental import pallas as pl
from jax.experimental.pallas import tpu as pltpu
from jax.sharding import PartitionSpec as P

LOOK_AZ = 4
LOOK_RG = 16
WIN = 5
SPAN = 5
GROUP = 8
FIELDS = 3 * SPAN + 1
SUB = 16


def cut_kernel(slab_ref, out_ref):
    planes, lines, _ = slab_ref.shape
    width = out_ref.shape[-1]
    for plane in range(planes):
        for line in range(0, lines, 8):
            for block in range(SUB):
                part = slab_ref[plane, line : line + 8, block * width : (block + 1) * width]
                start = (line * planes + plane) * SUB + block
                out_ref[pl.ds(start, 8, stride=planes * SUB), :] = part


def cut(slab):
    planes, lines, samples = slab.shape
    rows = planes * lines * SUB
    return pl.pallas_call(
        cut_kernel,
        out_shape=jax.ShapeDtypeStruct((rows, samples // SUB), jnp.float32),
        compiler_params=pltpu.CompilerParams(vmem_limit_bytes=4 * 1024 * 1024),
        name="cut",
    )(slab)


def look_kernel(own_ref, later_ref, out_ref, sums, cells):
    width = own_ref.shape[-1]

    def date(index):
        ref, at = (own_ref, index) if index < GROUP else (later_ref, index - GROUP)
        return [ref[at, 2 * k] for k in range(LOOK_AZ)], [ref[at, 2 * k + 1] for k in range(LOOK_AZ)]

    def put(row, terms):
        total = terms[0]
        for term in terms[1:]:
            total = total + term
        sums[row * SUB : (row + 1) * SUB, :] = total

    first_power = 2 * SPAN * GROUP
    for index in range(GROUP + SPAN):
        real, imag = date(index)
        put(first_power + index, [v * v for v in real + imag])
        if index >= GROUP:
            continue
        for gap in range(1, SPAN + 1):
            other_real, other_imag = date(index + gap)
            row = index * 2 * SPAN + gap - 1
            put(row, [a * b for a, b in zip(real + imag, other_real + other_imag)])
            put(row + SPAN, [a * b - c * d for a, b, c, d in zip(imag, other_real, real, other_imag)])

    cols = cells.shape[-1]
    per_block = width // LOOK_RG
    sample = lax.broadcasted_iota(jnp.int32, (width, cols), 0)
    lane = lax.broadcasted_iota(jnp.int32, (width, cols), 1)
    weight = jnp.where(sample // LOOK_RG == lane % per_block, 1.0 / (LOOK_AZ * LOOK_RG), 0.0)
    looks = jnp.dot(sums[...], weight, precision=lax.Precision.HIGHEST, preferred_element_type=jnp.float32)
    looks = looks.reshape(looks.shape[0] // SUB, SUB, cols)
    block = lax.broadcasted_iota(jnp.int32, (1, SUB, cols), 1)
    lane = lax.broadcasted_iota(jnp.int32, (1, SUB, cols), 2)
    cells[...] = jnp.sum(jnp.where(lane // per_block == block, looks, 0.0), axis=1)
    for index in range(GROUP):
        cross = cells[index * 2 * SPAN : (index + 1) * 2 * SPAN, :]
        power = cells[first_power + index : first_power + index + SPAN + 1, :]
        for tile in range(out_ref.shape[1]):
            out_ref[index, tile, : 2 * SPAN, :] = cross
            out_ref[index, tile, 2 * SPAN :, :] = power


def look(own, later, tiles, cols):
    rows = 2 * SPAN * GROUP + GROUP + SPAN
    return pl.pallas_call(
        look_kernel,
        out_shape=jax.ShapeDtypeStruct((GROUP, tiles, FIELDS, cols), jnp.float32),
        scratch_shapes=[
            pltpu.VMEM((rows * SUB, own.shape[-1]), jnp.float32),
            pltpu.VMEM((rows, cols), jnp.float32),
        ],
        compiler_params=pltpu.CompilerParams(vmem_limit_bytes=8 * 1024 * 1024),
        name="look",
    )(own, later)


def coherence_kernel(rows_ref, looks_ref, coher_ref):
    date, dates = lax.axis_index("date"), lax.axis_size("date")
    tile = lax.axis_index("az")
    tiles, cols = rows_ref.shape[1], rows_ref.shape[-1]
    half = WIN // 2
    lane = lax.broadcasted_iota(jnp.int32, (FIELDS, cols), 1)
    rows = []
    for offset in range(-half, GROUP + half):
        other = tile + offset // GROUP
        inside = jnp.logical_and(other >= 0, other < tiles)
        row = rows_ref[offset % GROUP, jnp.clip(other, 0, tiles - 1)]
        rows.append(row if 0 <= offset < GROUP else jnp.where(inside, row, 0.0))
    for r in range(GROUP):
        tall = rows[r]
        for shift in range(1, WIN):
            tall = tall + rows[r + shift]
        boxed = tall
        for shift in range(1, half + 1):
            boxed = boxed + jnp.where(lane >= shift, pltpu.roll(tall, shift, 1), 0.0)
            boxed = boxed + jnp.where(lane < cols - shift, pltpu.roll(tall, cols - shift, 1), 0.0)
        real = boxed[:SPAN]
        imag = boxed[SPAN : 2 * SPAN]
        own = boxed[2 * SPAN : 2 * SPAN + 1]
        later = boxed[2 * SPAN + 1 :]
        value = jnp.sqrt(real * real + imag * imag) / jnp.sqrt(own * later + 1e-06)
        for gap in range(1, SPAN + 1):
            paired = date + gap < dates
            coher_ref[gap - 1, 0, r : r + 1, :] = jnp.where(paired, value[gap - 1 : gap], 0.0)
            for part in range(2):
                field = part * SPAN + gap - 1
                looks_ref[gap - 1, part, 0, r : r + 1, :] = jnp.where(paired, rows[r + half][field : field + 1], 0.0)


def finish(rows):
    cols = rows.shape[-1]
    return pl.pallas_call(
        coherence_kernel,
        out_shape=(
            jax.ShapeDtypeStruct((SPAN, 2, 1, GROUP, cols), jnp.float32),
            jax.ShapeDtypeStruct((SPAN, 1, GROUP, cols), jnp.float32),
        ),
        compiler_params=pltpu.CompilerParams(vmem_limit_bytes=4 * 1024 * 1024),
        name="finish",
    )(rows)


def local(slabs):
    dates, tiles = lax.axis_size("date"), lax.axis_size("az")
    _, planes, lines, samples = slabs.shape
    cols = samples // LOOK_RG
    groups = [list(range(g, g + GROUP)) for g in range(0, dates, GROUP)]
    wide = [list(range(g * tiles, (g + GROUP) * tiles)) for g in range(0, dates, GROUP)]
    pieces = cut(slabs[0]).reshape(GROUP, LOOK_AZ * planes, SUB, samples // SUB)
    own = lax.all_to_all(pieces, "date", 0, 0, axis_index_groups=groups, tiled=True)
    back = [(i, (i - GROUP) % dates) for i in range(dates)]
    later = lax.ppermute(own[:SPAN], "date", back)
    fields = look(own, later, tiles, cols)
    fields = fields.reshape(GROUP * tiles, FIELDS, cols)
    rows = lax.all_to_all(fields, ("date", "az"), 0, 0, axis_index_groups=wide, tiled=True)
    return finish(rows.reshape(GROUP, tiles, FIELDS, cols))


def solution(mesh):
    in_specs = (P("date", None, "az", None),)
    out_specs = (P(None, None, "date", "az", None), P(None, "date", "az", None))
    return jax.shard_map(local, mesh=mesh, in_specs=in_specs, out_specs=out_specs, check_vma=False)
```

profile of v0, /device:TPU:1, one launch (start us, length us, event | category | flops | bytes accessed | tf_op | source)
XLA Modules:
  0.0 50.8 jit_solution(8048000507726585042)
XLA Ops:
  0.6 0.0 copy-start
  0.6 1.0 %copy-done = f32[1,2,32,2048]{3,2,1,0:T(8,128)S(1)} copy-done((f32[1,2,32,2048]{3,2,1,0:T(8,128)S(1)}, f32[1,2,32,2048]{3,2,1,0:T(8,128)}, u32[]{:S(2)}) %copy-start) | copy-done | bytes 524312
  1.7 0.3 cut.1
  2.0 13.3 %all_to_all.10.own_ref = f32[8,8,16,128]{3,2,1,0:T(8,128)S(1)} all-to-all(f32[8,8,16,128]{3,2,1,0:T(8,128)S(1)} %bitcast.4), channel_id=1, replica_groups={{0,4,8,12,16,20,24,28},{32,36,40,44,48,52,56,60},{64,68,72,76,80,84,88,..., dimensions={0} | all-to-all | bytes 1048576 | tf_op jit(solution)/shard_map/all_to_all | solution.py:149
  15.3 12.8 %collective-permute-start = (f32[5,8,16,128]{3,2,1,0:T(8,128)S(1)}, f32[5,8,16,128]{3,2,1,0:T(8,128)S(1)}, u32[]{:S(2)}, u32[]{:S(2)}) collective-permute-start(f32[5,8,16,128]{3,2,1,0:T(8,128)S(1)} %slice.4), channel_id=1, source_target_pairs={{0,480},{4,484},{8,488},{12,492},{16,496},{20,500},{24,504},{28,50... | collective-permute-start | bytes 983048 | tf_op jit(solution)/shard_map/ppermute | solution.py:151
  28.1 5.1 %collective-permute-done.later_ref = f32[5,8,16,128]{3,2,1,0:T(8,128)S(1)} collective-permute-done((f32[5,8,16,128]{3,2,1,0:T(8,128)S(1)}, f32[5,8,16,128]{3,2,1,0:T(8,128)S(1)}, u32[]{:S(2)}, u32[]{:S(2)}) %collective-permute-start) | collective-permute-done | bytes 327712 | tf_op jit(solution)/shard_map/ppermute | solution.py:151
  33.2 1.1 %look.1 = f32[8,4,16,128]{3,2,1,0:T(8,128)S(1)} custom-call(f32[8,8,16,128]{3,2,1,0:T(8,128)S(1)} %all_to_all.10.own_ref, f32[5,8,16,128]{3,2,1,0:T(8,128)S(1)} %collective-permute-done.later_ref), custom_call_target="tpu_custom_call" | custom-call | tf_op jit(solution)/shard_map/look/pallas_call | solution.py:84
  34.3 15.7 %all_to_all.11 = f32[32,16,128]{2,1,0:T(8,128)S(1)} all-to-all(f32[32,16,128]{2,1,0:T(8,128)S(1)} %bitcast.5), channel_id=1, replica_groups={{0,1,2,3,4,5,6,7,8,9,10,11,12,13,14,15,16,17,18,19,20,21,22,23,24,25,26..., dimensions={0} | all-to-all | bytes 524288 | tf_op jit(solution)/shard_map/all_to_all | solution.py:154
  50.0 0.8 %finish.1 = (f32[5,2,1,8,128]{4,3,2,1,0:T(8,128)}, f32[5,1,8,128]{3,2,1,0:T(8,128)}) custom-call(f32[8,4,16,128]{3,2,1,0:T(8,128)S(1)} %bitcast.6), custom_call_target="tpu_custom_call" | custom-call | tf_op jit(solution)/shard_map/finish/pallas_call | solution.py:131
  (1 shorter events, 0.0 us)
Async XLA Ops:
  0.6 1.0 %copy-start = (f32[1,2,32,2048]{3,2,1,0:T(8,128)S(1)}, f32[1,2,32,2048]{3,2,1,0:T(8,128)}, u32[]{:S(2)}) copy-start(f32[1,2,32,2048]{3,2,1,0:T(8,128)} %param.1) | copy-start | bytes 1572868
  15.3 17.9 %collective-permute-start = (f32[5,8,16,128]{3,2,1,0:T(8,128)S(1)}, f32[5,8,16,128]{3,2,1,0:T(8,128)S(1)}, u32[]{:S(2)}, u32[]{:S(2)}) collective-permute-start(f32[5,8,16,128]{3,2,1,0:T(8,128)S(1)} %slice.4), channel_id=1, source_target_pairs={{0,480},{4,484},{8,488},{12,492},{16,496},{20,500},{24,504},{28,50... | collective-permute-start | bytes 983048 | tf_op jit(solution)/shard_map/ppermute | solution.py:151
where the time goes:
time: 51 us; the launch traced here: 50.8 us
  blocking collectives  28.9 us (57%)
  starting transfers between devices  12.8 us (25%)
  waiting for transfers between devices  5.12 us (10%)
  Pallas kernels  2.18 us (4%)
  local copies, waits for them, and re-layouts  1.06 us (2%)
  between operations  0.66 us (1%)
    all_to_all x1, blocking collectives, local(): lax.all_to_all(fields, ('date', 'az'), 0, 0, axis_index_groups=wide, tile...  15.7 us
    all_to_all x1, blocking collectives, local(): lax.all_to_all(pieces, 'date', 0, 0, axis_index_groups=groups, tiled=True)  13.3 us
    ppermute x1, starting transfers between devices, local(): later = lax.ppermute(own[:SPAN], 'date', back)  12.8 us
    ppermute x1, waiting for transfers between devices, local(): later = lax.ppermute(own[:SPAN], 'date', back)  5.12 us
    pallas_call x1, Pallas kernels, look(): pl.pallas_call(look_kernel, out_shape=jax.ShapeDtypeStruct((GROUP, tiles,...  1.09 us
    unnamed x2, local copies, waits for them, and re-layouts  1.03 us
  transfers between devices with their start and end apart: 1, of which 1 were waited for; matrix products, arithmetic and copies ran while one was open for 0% of the time, Pallas kernels for 0%

commit v1 on v0

--- a/solution.py
+++ b/solution.py
@@ -36,61 +36,110 @@
     )(slab)
 
 
-def look_kernel(own_ref, later_ref, out_ref, sums, cells):
-    width = own_ref.shape[-1]
-
-    def date(index):
-        ref, at = (own_ref, index) if index < GROUP else (later_ref, index - GROUP)
-        return [ref[at, 2 * k] for k in range(LOOK_AZ)], [ref[at, 2 * k + 1] for k in range(LOOK_AZ)]
-
-    def put(row, terms):
+def inside(index):
+    return min(SPAN, GROUP - 1 - index)
+
+
+def look_at(date, pairs, powers, sums, cols):
+    width = sums.shape[-1]
+    count = 0
+
+    def put(terms):
+        nonlocal count
         total = terms[0]
         for term in terms[1:]:
             total = total + term
-        sums[row * SUB : (row + 1) * SUB, :] = total
-
-    first_power = 2 * SPAN * GROUP
-    for index in range(GROUP + SPAN):
+        sums[count * SUB : (count + 1) * SUB, :] = total
+        count += 1
+
+    for index, gaps in pairs:
         real, imag = date(index)
-        put(first_power + index, [v * v for v in real + imag])
-        if index >= GROUP:
-            continue
-        for gap in range(1, SPAN + 1):
-            other_real, other_imag = date(index + gap)
-            row = index * 2 * SPAN + gap - 1
-            put(row, [a * b for a, b in zip(real + imag, other_real + other_imag)])
-            put(row + SPAN, [a * b - c * d for a, b, c, d in zip(imag, other_real, real, other_imag)])
-
-    cols = cells.shape[-1]
+        others = [date(index + gap) for gap in gaps]
+        for other_real, other_imag in others:
+            put([a * b for a, b in zip(real + imag, other_real + other_imag)])
+        for other_real, other_imag in others:
+            put([a * b - c * d for a, b, c, d in zip(imag, other_real, real, other_imag)])
+    for index in powers:
+        real, imag = date(index)
+        put([v * v for v in real + imag])
+
     per_block = width // LOOK_RG
     sample = lax.broadcasted_iota(jnp.int32, (width, cols), 0)
     lane = lax.broadcasted_iota(jnp.int32, (width, cols), 1)
     weight = jnp.where(sample // LOOK_RG == lane % per_block, 1.0 / (LOOK_AZ * LOOK_RG), 0.0)
-    looks = jnp.dot(sums[...], weight, precision=lax.Precision.HIGHEST, preferred_element_type=jnp.float32)
-    looks = looks.reshape(looks.shape[0] // SUB, SUB, cols)
+    looks = jnp.dot(
+        sums[: count * SUB, :], weight, precision=lax.Precision.HIGHEST, preferred_element_type=jnp.float32
+    )
+    looks = looks.reshape(count, SUB, cols)
     block = lax.broadcasted_iota(jnp.int32, (1, SUB, cols), 1)
     lane = lax.broadcasted_iota(jnp.int32, (1, SUB, cols), 2)
-    cells[...] = jnp.sum(jnp.where(lane // per_block == block, looks, 0.0), axis=1)
+    return jnp.sum(jnp.where(lane // per_block == block, looks, 0.0), axis=1)
+
+
+def planes_of(ref, at):
+    return [ref[at, 2 * k] for k in range(LOOK_AZ)], [ref[at, 2 * k + 1] for k in range(LOOK_AZ)]
+
+
+OWN_PAIRS = [(d, range(1, inside(d) + 1)) for d in range(GROUP)]
+LATER_PAIRS = [(d, range(inside(d) + 1, SPAN + 1)) for d in range(GROUP) if inside(d) < SPAN]
+OWN_ROWS = sum(2 * len(gaps) for _, gaps in OWN_PAIRS)
+LATER_ROWS = sum(2 * len(gaps) for _, gaps in LATER_PAIRS)
+
+
+def own_kernel(own_ref, out_ref, sums):
+    out_ref[...] = look_at(lambda d: planes_of(own_ref, d), OWN_PAIRS, range(GROUP), sums, out_ref.shape[-1])
+
+
+def later_kernel(own_ref, later_ref, looks_ref, out_ref, sums, cells):
+    def date(index):
+        return planes_of(own_ref, index) if index < GROUP else planes_of(later_ref, index - GROUP)
+
+    cells[...] = look_at(date, LATER_PAIRS, range(GROUP, GROUP + SPAN), sums, out_ref.shape[-1])
+    own_at = later_at = 0
     for index in range(GROUP):
-        cross = cells[index * 2 * SPAN : (index + 1) * 2 * SPAN, :]
-        power = cells[first_power + index : first_power + index + SPAN + 1, :]
-        for tile in range(out_ref.shape[1]):
-            out_ref[index, tile, : 2 * SPAN, :] = cross
-            out_ref[index, tile, 2 * SPAN :, :] = power
-
-
-def look(own, later, tiles, cols):
-    rows = 2 * SPAN * GROUP + GROUP + SPAN
-    return pl.pallas_call(
-        look_kernel,
+        near, far = inside(index), SPAN - inside(index)
+        piece = out_ref.at[index, 0]
+        for part in range(2):
+            if near:
+                piece[part * SPAN : part * SPAN + near, :] = looks_ref[own_at : own_at + near, :]
+            if far:
+                piece[part * SPAN + near : (part + 1) * SPAN, :] = cells[later_at : later_at + far, :]
+            own_at += near
+            later_at += far
+        piece[2 * SPAN : 2 * SPAN + 1 + near, :] = looks_ref[OWN_ROWS + index : OWN_ROWS + index + 1 + near, :]
+        if far:
+            piece[2 * SPAN + 1 + near :, :] = cells[LATER_ROWS : LATER_ROWS + far, :]
+        for tile in range(1, out_ref.shape[1]):
+            out_ref[index, tile] = out_ref[index, 0]
+
+
+def look_own(own, cols):
+    rows = OWN_ROWS + GROUP
+    return pl.pallas_call(
+        own_kernel,
+        out_shape=jax.ShapeDtypeStruct((rows, cols), jnp.float32),
+        scratch_shapes=[pltpu.VMEM((rows * SUB, own.shape[-1]), jnp.float32)],
+        compiler_params=pltpu.CompilerParams(vmem_limit_bytes=8 * 1024 * 1024),
+        cost_estimate=pl.CostEstimate(
+            flops=12 * rows * SUB * cols * cols, bytes_accessed=own.size * 4, transcendentals=0
+        ),
+        name="look_own",
+    )(own)
+
+
+def look_later(own, later, looks, tiles):
+    cols = looks.shape[-1]
+    rows = LATER_ROWS + SPAN
+    return pl.pallas_call(
+        later_kernel,
         out_shape=jax.ShapeDtypeStruct((GROUP, tiles, FIELDS, cols), jnp.float32),
         scratch_shapes=[
             pltpu.VMEM((rows * SUB, own.shape[-1]), jnp.float32),
             pltpu.VMEM((rows, cols), jnp.float32),
         ],
         compiler_params=pltpu.CompilerParams(vmem_limit_bytes=8 * 1024 * 1024),
-        name="look",
-    )(own, later)
+        name="look_later",
+    )(own, later, looks)
 
 
 def coherence_kernel(rows_ref, looks_ref, coher_ref):
@@ -147,9 +196,9 @@
     wide = [list(range(g * tiles, (g + GROUP) * tiles)) for g in range(0, dates, GROUP)]
     pieces = cut(slabs[0]).reshape(GROUP, LOOK_AZ * planes, SUB, samples // SUB)
     own = lax.all_to_all(pieces, "date", 0, 0, axis_index_groups=groups, tiled=True)
-    back = [(i, (i - GROUP) % dates) for i in range(dates)]
+    back = [(i, i - GROUP) for i in range(GROUP, dates)]
     later = lax.ppermute(own[:SPAN], "date", back)
-    fields = look(own, later, tiles, cols)
+    fields = look_later(own, later, look_own(own, cols), tiles)
     fields = fields.reshape(GROUP * tiles, FIELDS, cols)
     rows = lax.all_to_all(fields, ("date", "az"), 0, 0, axis_index_groups=wide, tiled=True)
     return finish(rows.reshape(GROUP, tiles, FIELDS, cols))

time: 51 us -> 44 us (0.86)
  starting transfers between devices: 12.8 us -> 1.29 us
  waiting for transfers between devices: 5.12 us -> 8.09 us
  blocking collectives: 28.9 us -> 29.9 us
    ppermute x1, starting transfers between devices: 12.8 us -> 1.29 us  [local(): later = lax.ppermute(own[:SPAN], 'date', back)]
    ppermute x1, waiting for transfers between devices: 5.12 us -> 8.09 us  [local(): later = lax.ppermute(own[:SPAN], 'date', back)]
    all_to_all x1, blocking collectives: 15.7 us -> 16.6 us  [local(): lax.all_to_all(fields, ('date', 'az'), 0, 0, axis_index_groups=wide, tile...]
    pallas_call x1 -> x2, Pallas kernels: 1.09 us -> 1.25 us  [the longest x1 0.73 us: look_own(): pl.pallas_call(own_kernel, out_shape=jax.ShapeDtypeStruct((rows, cols), j...]
  transfers between devices with their start and end apart: 1 -> 1, of which waited for: 1 -> 1; matrix products, arithmetic and copies ran while one was open for 0% -> 0% of each run, Pallas kernels for 0% -> 2%
where the time goes in v1:
time: 44 us; the launch traced here: 43.4 us
  blocking collectives  29.9 us (68%)
  waiting for transfers between devices  8.09 us (18%)
  Pallas kernels  2.33 us (5%)
  starting transfers between devices  1.29 us (3%)
  local copies, waits for them, and re-layouts  1.06 us (2%)
  between operations  0.67 us (2%)
    all_to_all x1, blocking collectives, local(): lax.all_to_all(fields, ('date', 'az'), 0, 0, axis_index_groups=wide, tile...  16.6 us
    all_to_all x1, blocking collectives, local(): lax.all_to_all(pieces, 'date', 0, 0, axis_index_groups=groups, tiled=True)  13.3 us
    ppermute x1, waiting for transfers between devices, local(): later = lax.ppermute(own[:SPAN], 'date', back)  8.09 us
    ppermute x1, starting transfers between devices, local(): later = lax.ppermute(own[:SPAN], 'date', back)  1.29 us
    unnamed x2, local copies, waits for them, and re-layouts  1.03 us
  transfers between devices with their start and end apart: 1, of which 1 were waited for; matrix products, arithmetic and copies ran while one was open for 0% of the time, Pallas kernels for 2%

profile of v1, /device:TPU:1, one launch (start us, length us, event | category | flops | bytes accessed | tf_op | source)
XLA Modules:
  0.0 43.4 jit_solution(7273905825816705956)
XLA Ops:
  0.6 0.0 copy-start
  0.6 1.0 %copy-done = f32[1,2,32,2048]{3,2,1,0:T(8,128)S(1)} copy-done((f32[1,2,32,2048]{3,2,1,0:T(8,128)S(1)}, f32[1,2,32,2048]{3,2,1,0:T(8,128)}, u32[]{:S(2)}) %copy-start) | copy-done | bytes 524312
  1.7 0.3 cut.1
  2.0 13.3 %all_to_all.10.own_ref = f32[8,8,16,128]{3,2,1,0:T(8,128)S(1)} all-to-all(f32[8,8,16,128]{3,2,1,0:T(8,128)S(1)} %bitcast.4), channel_id=1, replica_groups={{0,4,8,12,16,20,24,28},{32,36,40,44,48,52,56,60},{64,68,72,76,80,84,88,..., dimensions={0} | all-to-all | bytes 1048576 | tf_op jit(solution)/shard_map/all_to_all | solution.py:198
  15.3 1.3 %collective-permute-start = (f32[5,8,16,128]{3,2,1,0:T(8,128)S(1)}, f32[5,8,16,128]{3,2,1,0:T(8,128)S(1)}, u32[]{:S(2)}, u32[]{:S(2)}) collective-permute-start(f32[5,8,16,128]{3,2,1,0:T(8,128)S(1)} %slice.4), channel_id=1, source_target_pairs={{32,0},{36,4},{40,8},{44,12},{48,16},{52,20},{56,24},{60,28},{64,3... | collective-permute-start | bytes 983048 | tf_op jit(solution)/shard_map/ppermute | solution.py:200
  16.6 0.7 %look_own.1.looks_ref = f32[58,128]{1,0:T(8,128)S(1)} custom-call(f32[8,8,16,128]{3,2,1,0:T(8,128)S(1)} %all_to_all.10.own_ref), custom_call_target="tpu_custom_call" | custom-call | flops 182452224 | bytes 524288 | tf_op jit(solution)/shard_map/look_own/pallas_call | solution.py:118
  17.3 8.1 %collective-permute-done.later_ref = f32[5,8,16,128]{3,2,1,0:T(8,128)S(1)} collective-permute-done((f32[5,8,16,128]{3,2,1,0:T(8,128)S(1)}, f32[5,8,16,128]{3,2,1,0:T(8,128)S(1)}, u32[]{:S(2)}, u32[]{:S(2)}) %collective-permute-start) | collective-permute-done | bytes 327712 | tf_op jit(solution)/shard_map/ppermute | solution.py:200
  25.4 0.5 %look_later.1 = f32[8,4,16,128]{3,2,1,0:T(8,128)S(1)} custom-call(f32[8,8,16,128]{3,2,1,0:T(8,128)S(1)} %all_to_all.10.own_ref, f32[5,8,16,128]{3,2,1,0:T(8,128)S(1)} %collective-permute-done.later_ref, f32[58,128]{1,0:T(8,128)S(1)} %look_own.1.looks_ref), custom_call_target="tpu_custom_call" | custom-call | tf_op jit(solution)/shard_map/look_later/pallas_call | solution.py:133
  25.9 16.6 %all_to_all.11 = f32[32,16,128]{2,1,0:T(8,128)S(1)} all-to-all(f32[32,16,128]{2,1,0:T(8,128)S(1)} %bitcast.6), channel_id=1, replica_groups={{0,1,2,3,4,5,6,7,8,9,10,11,12,13,14,15,16,17,18,19,20,21,22,23,24,25,26..., dimensions={0} | all-to-all | bytes 524288 | tf_op jit(solution)/shard_map/all_to_all | solution.py:203
  42.6 0.8 %finish.1 = (f32[5,2,1,8,128]{4,3,2,1,0:T(8,128)}, f32[5,1,8,128]{3,2,1,0:T(8,128)}) custom-call(f32[8,4,16,128]{3,2,1,0:T(8,128)S(1)} %bitcast.5), custom_call_target="tpu_custom_call" | custom-call | tf_op jit(solution)/shard_map/finish/pallas_call | solution.py:180
  (1 shorter events, 0.0 us)
Async XLA Ops:
  0.6 1.0 %copy-start = (f32[1,2,32,2048]{3,2,1,0:T(8,128)S(1)}, f32[1,2,32,2048]{3,2,1,0:T(8,128)}, u32[]{:S(2)}) copy-start(f32[1,2,32,2048]{3,2,1,0:T(8,128)} %param.1) | copy-start | bytes 1572868
  15.3 10.1 %collective-permute-start = (f32[5,8,16,128]{3,2,1,0:T(8,128)S(1)}, f32[5,8,16,128]{3,2,1,0:T(8,128)S(1)}, u32[]{:S(2)}, u32[]{:S(2)}) collective-permute-start(f32[5,8,16,128]{3,2,1,0:T(8,128)S(1)} %slice.4), channel_id=1, source_target_pairs={{32,0},{36,4},{40,8},{44,12},{48,16},{52,20},{56,24},{60,28},{64,3... | collective-permute-start | bytes 983048 | tf_op jit(solution)/shard_map/ppermute | solution.py:200
